TPU v7x, 128 devices: a whole 4x4x4 slice. The times are simulated.
128 devices in a mesh: tok: 32 (over z, y, x_hi), row: 2 (over x_lo), col: 2 (over core).
Axes of the slice: x: 4 (x_hi: 2, x_lo: 2; x = x_hi * 2 + x_lo), y: 4, z: 4, core: 2. Of those that a mesh axis runs over, the one named last changes fastest.
Arguments:
- tokens: bfloat16 [960, 16384], P('row', ('tok', 'col')), may hold values from -6 to 6
- gain_attn: float32 [960], P('row'), may hold values from 0.5 to 1.5
- gain_mlp: float32 [960], P('row'), may hold values from 0.5 to 1.5
- w_query: bfloat16 [960, 960], P('row', 'col'), may hold values from -0.1875 to 0.1875
- w_key: bfloat16 [960, 320], P('row', 'col'), may hold values from -0.1875 to 0.1875
- w_value: bfloat16 [960, 320], P('row', 'col'), may hold values from -0.1875 to 0.1875
- w_out: bfloat16 [960, 960], P('col', 'row'), may hold values from -0.75 to 0.75
- w_gate: bfloat16 [960, 2560], P('row', 'col'), may hold values from -0.1875 to 0.1875
- w_up: bfloat16 [960, 2560], P('row', 'col'), may hold values from -0.1875 to 0.1875
- w_down: bfloat16 [960, 2560], P('row', 'col'), may hold values from -0.25 to 0.25
- seq_lengths: int32 [128, 3], P(('tok', 'row', 'col')), may hold values from 1 to 96, 128 in all within a row
- cotangent: float32 [960, 16384], P('row', ('tok', 'col')), may hold values from -6 to 6
Outputs:
- output: float32 [960, 16384], P('row', ('tok', 'col'))
- grad_tokens: float32 [960, 16384], P('row', ('tok', 'col'))
- grad_gain_attn: float32 [960], P('row')
- grad_gain_mlp: float32 [960], P('row')
- grad_w_query: float32 [960, 960], P('row', 'col')
- grad_w_key: float32 [960, 320], P('row', 'col')
- grad_w_value: float32 [960, 320], P('row', 'col')
- grad_w_out: float32 [960, 960], P('col', 'row')
- grad_w_gate: float32 [960, 2560], P('row', 'col')
- grad_w_up: float32 [960, 2560], P('row', 'col')
- grad_w_down: float32 [960, 2560], P('row', 'col')
Inputs may be any that keep to these rules, and one draw needn't show every extreme that they name: `seq_lengths`: row s holds the lengths of the 3 sequences of token shard s in order; each row sums to 128 and its largest entry is exactly 96.
All inputs are finite; a program needn't handle non-finite values.
Results may differ from a plain program's by a relative error of at most 0.025.
Values may be sent and summed in bfloat16 or wider, within the bound.
A program may use at most 128 MiB of HBM per device.

v0:
```python
import math

import jax
import jax.numpy as jnp
from jax import lax
from jax.experimental import pallas as pl
from jax.experimental.pallas import tpu as pltpu
from jax.sharding import PartitionSpec as P

MESH = pl.DeviceIdType.MESH
MIB = 1024 * 1024


def position():
    t = lax.axis_index("tok")
    r = lax.axis_index("row")
    c = lax.axis_index("col")
    return {"x": (t % 2) * 2 + r, "y": (t // 2) % 4, "z": t // 8, "c": c}


def device(place, axis, step):
    p = dict(place)
    p[axis] = (p[axis] + step) % (2 if axis == "c" else 4)
    return (p["z"] * 8 + p["y"] * 2 + p["x"] // 2, p["x"] % 2, p["c"])


def meet(place):
    barrier = pltpu.get_barrier_semaphore()
    partners = [("c", 1)] + [(a, d) for a in "xyz" for d in (1, 2, 3)]
    for axis, step in partners:
        pl.semaphore_signal(
            barrier, inc=1, device_id=device(place, axis, step), device_id_type=MESH
        )
    pl.semaphore_wait(barrier, len(partners))


def send(src, dst, send_sem, recv_sem, target):
    copy = pltpu.make_async_remote_copy(
        src_ref=src, dst_ref=dst, send_sem=send_sem, recv_sem=recv_sem,
        device_id=target, device_id_type=MESH,
    )
    copy.start()
    return copy


ROWS = 512
STREAMS = (
    ("down", 1280, "xyz"),
    ("gate", 1280, "yzx"),
    ("up", 1280, "zxy"),
    ("out", 512, "xyz"),
    ("q", 512, "yzx"),
    ("kv", 384, "zxy"),
)


def aligned(value, unit):
    return pl.multiple_of(value, unit)


class Stream:
    def __init__(self, order, place):
        self.order = order
        self.place = place

    def piece(self, acc, level, owner):
        size, start, lead = ROWS, 0, None
        for depth in range(level + 1):
            axis = self.order[depth]
            index = owner if depth == level else self.place[axis]
            if axis == "x":
                size //= 2
                start = start + (index // 2) * size
                lead = index % 2
            else:
                size //= 4
                start = start + index * size
        rows = pl.ds(aligned(start, 16), size)
        if lead is None:
            return acc.at[:, rows]
        return acc.at[lead, rows]

    def result(self, out, level):
        size, start = ROWS, 0
        for depth in range(level + 1):
            axis = self.order[depth]
            size //= 2 if axis == "x" else 4
            start = start + (self.place[axis] // 2 if axis == "x" else self.place[axis]) * size
        return out.at[pl.ds(aligned(start, 16), size)]

    def shape(self, level, n):
        size, lead = ROWS, 2
        for depth in range(level + 1):
            if self.order[depth] == "x":
                size //= 2
                lead = 1
            else:
                size //= 4
        return (lead, size, n) if lead == 2 else (size, n)


def add_rows(dst, srcs, step=16):
    shape = dst.shape
    if len(shape) == 2:
        views = [(dst, srcs)]
    else:
        views = [(dst.at[k], [s.at[k] for s in srcs]) for k in range(shape[0])]
    rows = shape[-2]
    step = min(step, rows)
    for d, ss in views:
        @pl.loop(0, rows // step)
        def _(i, d=d, ss=ss):
            at = pl.ds(aligned(i * step, step), step)
            total = d[at, :].astype(jnp.float32)
            for s in ss:
                total = total + s[at, :].astype(jnp.float32)
            d[at, :] = total.astype(d.dtype)


D = 960
HQ = 15
KVH = 5
HD = 64
EPS = 1e-05
THETA = 100000.0


def nn(left, right):
    return jnp.dot(left, right, preferred_element_type=jnp.float32)


def nt(left, right):
    return lax.dot_general(
        left, right, (((1,), (1,)), ((), ())), preferred_element_type=jnp.float32
    )


def low(value):
    return value.astype(jnp.bfloat16)


def tables(seq):
    first, second = seq[0:1, 0:1], seq[0:1, 0:1] + seq[0:1, 1:2]

    def segment(index):
        return (index >= first).astype(jnp.int32) + (index >= second).astype(jnp.int32)

    lane = lax.broadcasted_iota(jnp.int32, (1, 128), 1)
    seg_q = segment(lane)
    begin = jnp.where(seg_q == 0, 0, jnp.where(seg_q == 1, first, second))
    place = (lane - begin).astype(jnp.float32)
    ladder = lax.broadcasted_iota(jnp.int32, (32, 128), 0).astype(jnp.float32)
    angle = place * jnp.exp(ladder * (-2.0 * math.log(THETA) / HD))
    rows = lax.broadcasted_iota(jnp.int32, (128, 128), 0)
    lanes = lax.broadcasted_iota(jnp.int32, (128, 128), 1)
    seg_rows = (rows >= first).astype(jnp.int32) + (rows >= second).astype(jnp.int32)
    seg_lanes = (lanes >= first).astype(jnp.int32) + (lanes >= second).astype(jnp.int32)
    allowed = (seg_rows == seg_lanes) & (rows <= lanes)
    return jnp.cos(angle), jnp.sin(angle), allowed


def rotate(head, cosine, sine):
    a, b = head[:32], head[32:]
    return jnp.concatenate([a * cosine - b * sine, b * cosine + a * sine], axis=0)


def features_total(parts):
    return jnp.sum(parts[0], axis=0, keepdims=True) + jnp.sum(parts[1], axis=0, keepdims=True)


def inverse_rms(parts):
    return lax.rsqrt(features_total([p * p for p in parts]) / D + EPS)


def norm_back(resid, scale, gain, grad):
    weighted = [grad[r] * gain[r] for r in range(2)]
    inner = features_total([weighted[r] * resid[r] for r in range(2)]) / D
    grad_resid = [
        weighted[r] * scale - resid[r] * (scale * scale * scale * inner) for r in range(2)
    ]
    grad_gain = [jnp.sum(grad[r] * resid[r] * scale, axis=1, keepdims=True) for r in range(2)]
    return grad_resid, grad_gain

UNIT = 48
BLOCK = 480
QKV = 896
NAMES = [s[0] for s in STREAMS]
N_OF = {s[0]: s[1] for s in STREAMS}


def mega_kernel(*refs):
    k = 5
    src = refs[:k]
    tok, cot, seq, misc = refs[k : k + 4]
    refs = refs[k + 4 :]
    out_ref, g_tok_ref = refs[:2]
    result = dict(zip(NAMES, refs[2:8]))
    refs = refs[8:]
    full, refs = refs[:k], refs[k:]
    w_qkv, w_out, w_gate, w_up, w_down = full
    acc = dict(zip(("down", "gate", "up", "kv"), refs[:4]))
    refs = refs[4:]
    mate, refs = dict(zip(NAMES, refs[:6])), refs[6:]
    got = {name: refs[3 * i : 3 * i + 3] for i, name in enumerate(NAMES)}
    refs = refs[18:]
    (
        seq_in, seq_own, misc_all, tok_all, cot_all, n1t, flat, qkvt, q_rot, k_rot, v_rot, probs_ref,
        ctxt, midt, n2t, gate_ref, up_ref, hidden, gbt, g_gate, g_up, g_midt,
        gat, gan, g_ctx, g_qkvt, out_own, scales,
    ) = refs[:28]
    work = qkvt.at[0:D]
    (
        local_sem, x_send, x_recv, relay_send, relay_recv, wm_send, wm_recv, act_send, act_recv,
        mate_send, mate_recv, rs_send, rs_recv, ag_send, ag_recv, keep_sem, end_send, end_recv,
    ) = refs[28:]
    acc["out"] = w_up.at[:, 0:ROWS, 0:512]
    acc["q"] = w_up.at[:, 0:ROWS, 512:1024]
    stage = {
        "down": acc["gate"].at[:, 0:BLOCK],
        "gate": w_down.at[0],
        "up": w_down.at[1],
        "out": w_gate.at[0, :, 0:512],
        "q": w_gate.at[0, :, 512:1024],
        "kv": w_gate.at[1, :, 0:384],
    }

    place = position()
    r, c = place["x"] % 2, place["c"]
    t = lax.axis_index("tok")
    row_mate, diagonal = (t, 1 - r, c), (t, 1 - r, 1 - c)
    core_mate = device(place, "c", 1)
    barrier = pltpu.get_barrier_semaphore()
    partners = [core_mate] + [device(place, a, d) for a in "xyz" for d in (1, 2, 3)] + [diagonal]
    for target in partners:
        pl.semaphore_signal(barrier, inc=1, device_id=target, device_id_type=MESH)
    pl.semaphore_wait(barrier, len(partners))

    def spot(i, row, col):
        lead, base = (row, col) if i == 1 else (col, row)
        return full[i].at[lead, pl.ds(aligned(base * BLOCK, 16), BLOCK)]

    def part(i, row, col, unit):
        lead, base = (row, col) if i == 1 else (col, row)
        return full[i].at[lead, pl.ds(aligned(base * BLOCK + unit * UNIT, 16), UNIT)]

    late = []
    seq_copy = send(seq, seq_in, act_send.at[2], act_recv.at[2], diagonal)
    misc_copy = send(misc, misc_all.at[r], act_send.at[3], act_recv.at[3], row_mate)
    theirs = pl.ds(aligned((1 - r) * 128, 128), 128)
    mine = pl.ds(aligned(r * 128, 128), 128)
    tok_copy = send(tok.at[:, theirs], tok_all.at[r], act_send.at[0], act_recv.at[0], row_mate)
    locals_ = []

    def local(a, b, sem):
        copy = pltpu.make_async_copy(a, b, sem)
        copy.start()
        return copy

    tok_local = local(tok.at[:, mine], tok_all.at[r], local_sem.at[k])
    cot_local = local(cot.at[:, mine], cot_all.at[r], local_sem.at[k + 1])
    misc_local = local(misc, misc_all.at[r], local_sem.at[k + 2])
    x_in, w_local, w_mate = [], [], []
    for i in range(k):
        arrive = []
        for j, (step, unit) in enumerate(((1, place["y"]), (3, 4 + place["z"]), (1, 8), (3, 9))):
            rows = pl.ds(aligned(unit * UNIT, 16), UNIT)
            arrive.append(
                send(
                    src[i].at[rows], part(i, r, c, unit), x_send.at[i, j], x_recv.at[i, j],
                    device(place, "x", step),
                )
            )
        x_in.append(arrive)
        w_local.append(local(src[i], spot(i, r, c), local_sem.at[i]))
        w_mate.append(send(src[i], spot(i, r, c), wm_send.at[i, 0], wm_recv.at[i, 0], core_mate))
    cot_copy = send(cot.at[:, theirs], cot_all.at[r], act_send.at[1], act_recv.at[1], row_mate)

    relays, forwards = {}, {}

    def relay(i):
        copies = []
        for j, (axis, unit) in enumerate((("y", place["y"]), ("z", 4 + place["z"]))):
            x_in[i][j].wait_recv()
            piece = part(i, 1 - r, c, unit)
            for d in (2, 1, 3):
                copies.append(
                    send(
                        piece, piece, relay_send.at[i, j, d - 1], relay_recv.at[i, j, d - 1],
                        device(place, axis, d),
                    )
                )
        relays[i] = copies

    def forward(i):
        for copy in x_in[i][2:] + relays[i]:
            copy.wait_recv()
        block = spot(i, 1 - r, c)
        forwards[i] = send(block, block, wm_send.at[i, 1], wm_recv.at[i, 1], core_mate)

    def ready(i):
        w_local[i].wait()
        w_mate[i].wait_recv()
        forwards[i].wait_recv()

    def release(i):
        for copy in x_in[i] + relays[i] + [w_mate[i], forwards[i]]:
            copy.wait_send()

    streams = {name: Stream(order, place) for name, _, order in STREAMS}
    mates, flying, level_of, keep = {}, {}, {}, {}

    def to_mate(name):
        i = NAMES.index(name)
        mates[name] = send(stage[name], mate[name], mate_send.at[i], mate_recv.at[i], core_mate)

    def scatter(name, level):
        i, axis = NAMES.index(name), streams[name].order[level]
        flying[name] = [
            send(
                streams[name].piece(acc[name], level, (place[axis] + d) % 4), got[name][level].at[d - 1],
                rs_send.at[i, level, d - 1], rs_recv.at[i, level, d - 1], device(place, axis, d),
            )
            for d in (2, 1, 3)
        ]

    def spread(name, level, source=None):
        i, axis = NAMES.index(name), streams[name].order[level]
        there = streams[name].result(result[name], level)
        flying[name] = [
            send(
                there if source is None else source, there, ag_send.at[i, level, d - 1],
                ag_recv.at[i, level, d - 1], device(place, axis, d),
            )
            for d in ((2,) if axis == "x" else (2, 1, 3))
        ]

    def advance(name):
        step = level_of.get(name, 0)
        level_of[name] = step + 1
        i = NAMES.index(name)
        if step == 0:
            mates[name].wait_recv()
            for lead in range(2):
                theirs = mate[name].at[lead if name == "down" else pl.ds(lead * BLOCK, BLOCK)]
                add_rows(acc[name].at[lead, 0:BLOCK], [theirs])
            scatter(name, 0)
            return
        for copy in flying[name]:
            copy.wait()
        if step <= 3:
            level = step - 1
            own = streams[name].piece(acc[name], level, place[streams[name].order[level]])
            add_rows(own, [got[name][level].at[d] for d in range(3)])
            if level < 2:
                scatter(name, level + 1)
            else:
                keep[name] = local(own, streams[name].result(result[name], 2), keep_sem.at[i])
                spread(name, 2, own)
        elif step <= 5:
            if step == 4:
                keep[name].wait()
            spread(name, 5 - step)

    def wgrad(left, right_of, name, columns=256):
        n = N_OF[name]
        steps = -(-n // columns)

        def block(col, lanes, row):
            return low(nn(left[row * BLOCK : row * BLOCK + BLOCK, :], right_of(col, lanes)))

        def run(col, put):
            if n % columns == 0:
                @pl.loop(0, steps)
                def _(j):
                    lanes = pl.ds(aligned(j * columns, columns), columns)
                    for row in range(2):
                        put(row, lanes, block(col, lanes, row))
            else:
                for row in range(2):
                    put(row, pl.ds(0, n), block(col, pl.ds(0, n), row))

        def put_stage(row, lanes, value):
            if name == "down":
                stage[name][row, :, lanes] = value
            else:
                stage[name][row * BLOCK : row * BLOCK + BLOCK, lanes] = value

        def put_acc(row, lanes, value):
            acc[name][row, 0:BLOCK, lanes] = value

        run(1 - c, put_stage)
        to_mate(name)
        run(c, put_acc)
        for row in range(2):
            acc[name][row, BLOCK:ROWS, :] = jnp.zeros((ROWS - BLOCK, n), jnp.bfloat16)

    two = range(2)
    rows_of = [slice(row * BLOCK, row * BLOCK + BLOCK) for row in two]

    seq_copy.wait()
    seq_own[...] = jnp.where(r == c, seq[...], seq_in[...])
    cosine, sine, allowed = tables(seq_own[...])
    mask = jnp.concatenate([allowed] * 3, axis=1)
    misc_local.wait()
    misc_copy.wait()
    gains = [misc_all[row].T for row in two]
    gain_one = [gains[row][:BLOCK, 0:1] for row in two]
    gain_two = [gains[row][:BLOCK, 1:2] for row in two]
    tok_local.wait()
    tok_copy.wait()
    relay(0)
    relay(1)

    def resid(row):
        return tok_all[row].astype(jnp.float32)

    scales[0:1, :] = inverse_rms([resid(row) for row in two])
    for row in two:
        n1t[rows_of[row], :] = low(resid(row) * scales[0:1, :] * gain_one[row])
    flat[...] = n1t[...].T
    relay(2)
    forward(0)
    relay(3)
    ready(0)
    for col in two:
        both = nn(flat[...], w_qkv[col]).T
        qkvt[col * BLOCK : col * BLOCK + BLOCK, :] = both[:BLOCK]
        qkvt[960 + col * 160 : 1120 + col * 160, :] = both[480:640]
        qkvt[1280 + col * 160 : 1440 + col * 160, :] = both[640:800]
    relay(4)
    forward(1)
    for h in range(KVH):
        k_rot[h * 64 : h * 64 + 64, :] = low(rotate(qkvt[960 + h * 64 : 1024 + h * 64, :], cosine, sine))
        v_rot[h * 64 : h * 64 + 64, :] = low(qkvt[1280 + h * 64 : 1344 + h * 64, :])
        for j in range(3):
            at = (3 * h + j) * 64
            q_rot[h * 64 : h * 64 + 64, j * 128 : j * 128 + 128] = low(rotate(qkvt[at : at + 64, :], cosine, sine))
    for h in range(KVH):
        own = slice(h * 64, h * 64 + 64)
        scores = jnp.where(mask, nn(k_rot[own, :].T, q_rot[own, :]) * HD ** (-0.5), -1e30)
        expo = jnp.exp(scores - jnp.max(scores, axis=0, keepdims=True))
        probs = expo / jnp.sum(expo, axis=0, keepdims=True)
        probs_ref[h] = probs
        context = low(nn(v_rot[own, :], low(probs)))
        for j in range(3):
            at = (3 * h + j) * 64
            ctxt[at : at + 64, :] = context[:, j * 128 : j * 128 + 128]
        if h == 1:
            forward(2)
        if h == 3:
            forward(3)
    flat[...] = ctxt[...].T
    ready(1)
    for row in two:
        midt[rows_of[row], :] = resid(row) + nn(flat[...], w_out[row]).T
    forward(4)
    mids = [midt[rows_of[row], :] for row in two]
    scales[1:2, :] = inverse_rms(mids)
    for row in two:
        n2t[rows_of[row], :] = low(midt[rows_of[row], :] * scales[1:2, :] * gain_two[row])
    flat[...] = n2t[...].T
    ready(2)
    ready(3)

    @pl.loop(0, 10)
    def _(i):
        col = i // 5
        lanes = pl.ds(aligned(i % 5 * 256, 256), 256)
        gate = nn(flat[...], w_gate[col, :, lanes])
        up = nn(flat[...], w_up[col, :, lanes])
        gate_ref[col, :, lanes] = gate
        up_ref[col, :, lanes] = up
        hidden[col, :, lanes] = low(gate * jax.nn.sigmoid(gate) * up)

    cot_local.wait()
    cot_copy.wait()
    for row in two:
        gbt[rows_of[row], :] = low(cot_all[row])
    flat[...] = gbt[...].T
    wgrad(gbt, lambda col, lanes: hidden[col, :, lanes], "down")
    ready(4)

    @pl.loop(0, 10)
    def _(i):
        col = i // 5
        lanes = pl.ds(aligned(i % 5 * 256, 256), 256)
        grad = nn(flat[...], w_down[col, :, lanes])
        gate = gate_ref[col, :, lanes]
        sig = jax.nn.sigmoid(gate)
        g_gate[col, :, lanes] = low(grad * up_ref[col, :, lanes] * sig * (1.0 + gate * (1.0 - sig)))
        g_up[col, :, lanes] = low(grad * (gate * sig))

    advance("down")
    work[...] = midt[...]
    for col in two:
        work[...] += nt(w_down[col], hidden[col])
    out_own[...] = work[...]
    out_copy = send(
        out_own.at[pl.ds(aligned((1 - r) * BLOCK, 16), BLOCK)], out_ref.at[:, mine], end_send.at[0],
        end_recv.at[0], row_mate,
    )
    out_ref[:, mine] = out_own[pl.ds(aligned(r * BLOCK, 16), BLOCK), :]
    release(4)
    mates["down"].wait_send()
    wgrad(n2t, lambda col, lanes: g_gate[col, :, lanes], "gate")
    wgrad(n2t, lambda col, lanes: g_up[col, :, lanes], "up")
    advance("gate")
    work[...] = nt(w_gate[0], g_gate[0]) + nt(w_gate[1], g_gate[1])
    advance("up")
    work[...] += nt(w_up[0], g_up[0]) + nt(w_up[1], g_up[1])
    release(2)
    release(3)
    back, gain_two_grad = norm_back(
        [midt[rows_of[row], :] for row in two], scales[1:2, :], gain_two, [work[rows_of[row], :] for row in two]
    )
    for row in two:
        total = cot_all[row] + back[row]
        g_midt[rows_of[row], :] = total
        gat[rows_of[row], :] = low(total)
    gat[960:992, :] = jnp.zeros((32, 128), jnp.bfloat16)
    for row in two:
        gan[row] = gat[row * BLOCK : row * BLOCK + 512, :].T
    for col in two:
        at = slice(col * BLOCK, col * BLOCK + BLOCK)
        g_ctx[at, :] = low(
            nn(w_out[0, at, :], gat[0:BLOCK, :]) + nn(w_out[1, at, :], gat[BLOCK:960, :])
        )
    def out_block(col, row):
        left = ctxt[pl.ds(aligned(col * BLOCK, 16), BLOCK), :]
        return low(nn(left, gan[row]))

    for row in two:
        stage["out"][row * BLOCK : row * BLOCK + BLOCK, :] = out_block(1 - c, row)
    to_mate("out")
    for row in two:
        acc["out"][row, 0:BLOCK, :] = out_block(c, row)
        acc["out"][row, BLOCK:ROWS, :] = jnp.zeros((ROWS - BLOCK, 512), jnp.bfloat16)
    advance("down")
    for h in range(KVH):
        own = slice(h * 64, h * 64 + 64)
        g_cat = jnp.concatenate(
            [g_ctx[j * 64 : j * 64 + 64, :] for j in range(3 * h, 3 * h + 3)], axis=1
        )
        probs = probs_ref[h]
        g_v = low(nt(g_cat, low(probs)))
        g_probs = nn(v_rot[own, :].T, g_cat)
        g_scores = low(probs * (g_probs - jnp.sum(probs * g_probs, axis=0, keepdims=True)))
        g_q = nn(k_rot[own, :], g_scores) * HD ** (-0.5)
        g_k = low(rotate(nt(q_rot[own, :], g_scores) * HD ** (-0.5), cosine, -sine))
        parts = [(480, 160, h * 64, g_k), (640, 160, h * 64, g_v)]
        for j in range(3):
            g_j = low(rotate(g_q[:, j * 128 : j * 128 + 128], cosine, -sine))
            parts.append((0, 480, (3 * h + j) * 64, g_j))
        for base, width, at, value in parts:
            for half in two:
                row = at + 32 * half
                put = base + row % width
                g_qkvt[row // width, put : put + 32, :] = value[half * 32 : half * 32 + 32]
        if h == 1:
            advance("gate")
        if h == 2:
            advance("up")
    for col in two:
        g_qkvt[col, 800:QKV, :] = jnp.zeros((QKV - 800, 128), jnp.bfloat16)
    advance("out")
    work[0:BLOCK, :] = nn(w_qkv[0, 0:BLOCK, :], g_qkvt[0]) + nn(w_qkv[1, 0:BLOCK, :], g_qkvt[1])
    work[BLOCK:960, :] = nn(w_qkv[0, BLOCK:960, :], g_qkvt[0]) + nn(w_qkv[1, BLOCK:960, :], g_qkvt[1])
    back, gain_one_grad = norm_back(
        [resid(row) for row in two], scales[0:1, :], gain_one, [work[rows_of[row], :] for row in two]
    )
    for row in two:
        g_midt[rows_of[row], :] = g_midt[rows_of[row], :] + back[row]
    lane = lax.broadcasted_iota(jnp.int32, (BLOCK, 384), 1)

    def q_block(col, row):
        return low(nn(n1t[rows_of[row], :], g_qkvt[col, 0:512, :].T))

    def kv_block(col, row):
        value = nn(n1t[rows_of[row], :], g_qkvt[col, 480:864, :].T)
        value = jnp.where(lane == 320, gain_one_grad[row], value)
        return low(jnp.where(lane == 321, gain_two_grad[row], value))

    for name, block, n in (("q", q_block, 512), ("kv", kv_block, 384)):
        for row in two:
            stage[name][row * BLOCK : row * BLOCK + BLOCK, :] = block(1 - c, row)
        to_mate(name)
        for row in two:
            acc[name][row, 0:BLOCK, :] = block(c, row)
            acc[name][row, BLOCK:ROWS, :] = jnp.zeros((ROWS - BLOCK, n), jnp.bfloat16)
    g_copy = send(
        g_midt.at[pl.ds(aligned((1 - r) * BLOCK, 16), BLOCK)], g_tok_ref.at[:, mine], end_send.at[1],
        end_recv.at[1], row_mate,
    )
    g_tok_ref[:, mine] = g_midt[pl.ds(aligned(r * BLOCK, 16), BLOCK), :]
    advance("q")
    advance("kv")
    while any(level_of[name] < 7 for name in NAMES):
        for name in NAMES:
            if level_of[name] < 7:
                advance(name)
    out_copy.wait()
    g_copy.wait()
    for name in NAMES[1:]:
        mates[name].wait_send()
    release(0)
    release(1)


def run_layer(weights, tokens, cotangent, seq, misc):
    bf, f32 = jnp.bfloat16, jnp.float32
    dma = pltpu.SemaphoreType.DMA
    hbm, vmem = pl.BlockSpec(memory_space=pl.ANY), pl.BlockSpec(memory_space=pltpu.VMEM)
    place = {"x": 0, "y": 0, "z": 0, "c": 0}

    def v(shape, dtype=bf):
        return pltpu.VMEM(shape, dtype)

    scratch = [v((2, 2 * BLOCK, w.shape[1])) for w in weights]
    scratch += [v((2, ROWS, N_OF[name])) for name in ("down", "gate", "up", "kv")]
    scratch += [v((2, BLOCK, n) if name == "down" else (2 * BLOCK, n)) for name, n, _ in STREAMS]
    for _, n, order in STREAMS:
        for level in range(3):
            scratch.append(v((3,) + Stream(order, place).shape(level, n)))
    scratch += [
        v((8, 128), jnp.int32), v((8, 128), jnp.int32), v((2, 8, 512), f32), v((2, BLOCK, 128)),
        v((2, BLOCK, 128), f32), v((D, 128)), v((128, D)), v((1600, 128), f32), v((320, 384)),
        v((320, 128)), v((320, 128)), v((KVH, 128, 384), f32), v((D, 128)), v((D, 128), f32),
        v((D, 128)), v((2, 128, 1280), f32), v((2, 128, 1280), f32), v((2, 128, 1280)),
        v((D, 128)), v((2, 128, 1280)), v((2, 128, 1280)),
        v((D, 128), f32), v((992, 128)), v((2, 128, 512)), v((D, 128)), v((2, QKV, 128)), v((D, 128), f32),
        v((8, 128), f32),
    ]
    scratch += [
        dma((8,)), dma((5, 4)), dma((5, 4)), dma((5, 2, 3)), dma((5, 2, 3)), dma((5, 2)), dma((5, 2)),
        dma((4,)), dma((4,)), dma((6,)), dma((6,)), dma((6, 3, 3)), dma((6, 3, 3)), dma((6, 3, 3)),
        dma((6, 3, 3)), dma((6,)), dma((2,)), dma((2,)),
    ]
    return pl.pallas_call(
        mega_kernel,
        out_shape=[jax.ShapeDtypeStruct((BLOCK, 256), f32)] * 2
        + [jax.ShapeDtypeStruct((ROWS, n), bf) for _, n, _ in STREAMS],
        in_specs=[hbm] * 7 + [vmem] * 2,
        out_specs=[vmem] * 2 + [hbm] * 6,
        scratch_shapes=scratch,
        compiler_params=pltpu.CompilerParams(
            collective_id=1, has_side_effects=True, vmem_limit_bytes=63 * MIB
        ),
        cost_estimate=pl.CostEstimate(flops=8 * 10**9, bytes_accessed=60 * MIB, transcendentals=0),
    )(*weights, tokens, cotangent, seq, misc)


def on_device(
    tokens, gain_attn, gain_mlp, w_query, w_key, w_value, w_out, w_gate, w_up, w_down, seq_lengths, cotangent
):
    seq = jnp.pad(seq_lengths, ((0, 7), (0, 125)))
    misc = jnp.pad(jnp.stack([gain_attn, gain_mlp]), ((0, 6), (0, 32)))
    blank = jnp.zeros((BLOCK, QKV - 800), jnp.bfloat16)
    w_qkv = jnp.concatenate([w_query, w_key, w_value, blank], axis=1)
    out, g_tok, *sums = run_layer([w_qkv, w_out, w_gate, w_up, w_down], tokens, cotangent, seq, misc)
    f32 = {name: v[:BLOCK].astype(jnp.float32) for name, v in zip(NAMES, sums)}
    return (
        out, g_tok, f32["kv"][:, 320], f32["kv"][:, 321],
        f32["q"][:, :480], f32["kv"][:, :160], f32["kv"][:, 160:320], f32["out"][:, :480],
        f32["gate"], f32["up"], f32["down"],
    )

def solution(mesh):
    in_specs = (
        P("row", ("tok", "col")), P("row"), P("row"), P("row", "col"), P("row", "col"), P("row", "col"),
        P("col", "row"), P("row", "col"), P("row", "col"), P("row", "col"),
        P(("tok", "row", "col"), None), P("row", ("tok", "col")),
    )
    out_specs = (
        P("row", ("tok", "col")), P("row", ("tok", "col")), P("row"), P("row"), P("row", "col"),
        P("row", "col"), P("row", "col"), P("col", "row"), P("row", "col"), P("row", "col"), P("row", "col"),
    )
    return jax.shard_map(
        on_device, mesh=mesh, in_specs=in_specs, out_specs=out_specs, check_vma=False
    )
```

profile of v0, /device:TPU:0, one launch (start us, length us, event | category | flops | bytes accessed | tf_op | source)
XLA Modules:
  0.0 180.5 jit_solution(12659085284970182653)
XLA Ops:
  0.6 0.0 copy-start.7
  0.7 0.0 copy-start.6
  0.7 0.0 copy-start.8
  0.7 1.1 copy.27
  1.7 1.0 copy.28
  2.8 0.1 pad.15.clone
  2.9 2.2 %maximum_maximum_fusion.refs_0_ = bf16[480,896]{1,0:T(8,128)(2,1)} fusion(bf16[480,160]{1,0:T(8,128)(2,1)S(1)} %copy.28, bf16[480,160]{1,0:T(8,128)(2,1)S(1)} %copy.27, bf16[480,480]{1,0:T(8,128)(2,1)} %param.15, bf16[896]{0:T(1024)(128)(2,1)S(1)} %pad.15.clone), kind=kLoop, calls=%fused_computation.3 | loop fusion | flops 3440640 | bytes 1629952 | tf_op jit(solution)/shard_map/concatenate | solution.py:658
  5.1 0.0 copy-done.7
  5.1 0.0 copy-done.6
  5.1 0.6 select_maximum_fusion.refs_8_
  5.7 0.0 copy-done.8
  5.7 0.6 pad.8.refs_7_
  6.3 162.1 %shard_map.203 = (f32[480,256]{1,0:T(8,128)}, f32[480,256]{1,0:T(8,128)}, bf16[512,1280]{1,0:T(8,128)(2,1)}, bf16[512,1280]{1,0:T(8,128)(2,1)}, bf16[512,1280]{1...) custom-call(bf16[480,896]{1,0:T(8,128)(2,1)} %maximum_maximum_fusion.refs_0_, ...), custom_call_target="tpu_custom_call" | custom-call | flops 8000000000 | bytes 62914560 | tf_op jit(solution)/shard_map/pallas_call | solution.py:638
  168.4 0.0 copy-start.3
  168.4 0.0 copy-start.4
  168.4 4.3 %slice_convert_fusion = (f32[480,1280]{1,0:T(8,128)}, f32[480,1280]{1,0:T(8,128)}) fusion(bf16[512,1280]{1,0:T(8,128)(2,1)} %get-tuple-element.26, bf16[512,1280]{1,0:T(8,128)(2,1)} %get-tuple-element.25), kind=kLoop, calls=%fused_computation | loop fusion | flops 1228800 | bytes 7372800 | tf_op jit(solution)/shard_map/convert_element_type | solution.py:660
  172.8 0.0 copy-start.5
  172.8 0.0 copy-done.3
  172.8 0.0 copy-done.4
  172.8 1.5 slice_convert_fusion.3
  174.3 0.0 copy-done.5
  174.4 0.0 copy-start
  174.4 0.2 fusion
  174.6 0.9 copy.29
  175.5 0.9 copy.30
  176.4 0.9 slice_reduce_fusion
  177.3 0.0 copy-done
  177.3 0.0 copy-start.2
  177.3 0.0 copy-start.1
  177.3 1.6 slice_convert_fusion.2
  178.9 0.0 copy-done.2
  178.9 0.8 copy.33
  179.7 0.0 copy-done.1
  179.7 0.8 copy.34
  (2 shorter events, 0.1 us)
Async XLA Ops:
  0.6 4.4 %copy-start.7 = (f32[480]{0:T(512)S(1)}, f32[480]{0:T(512)}, u32[]{:S(2)}) copy-start(f32[480]{0:T(512)} %param.13) | copy-start | bytes 5764
  0.7 4.4 %copy-start.6 = (f32[480]{0:T(512)S(1)}, f32[480]{0:T(512)}, u32[]{:S(2)}) copy-start(f32[480]{0:T(512)} %param.14) | copy-start | bytes 5764
  0.7 5.1 %copy-start.8 = (s32[1,3]{1,0:T(1,128)S(1)}, s32[1,3]{1,0:T(1,128)}, u32[]{:S(2)}) copy-start(s32[1,3]{1,0:T(1,128)} %param.22) | copy-start | bytes 40
  168.4 4.3 %copy-start.3 = (bf16[512,512]{1,0:T(8,128)(2,1)S(1)}, bf16[512,512]{1,0:T(8,128)(2,1)}, u32[]{:S(2)}) copy-start(bf16[512,512]{1,0:T(8,128)(2,1)} %get-tuple-element.23) | copy-start | bytes 1572868
  168.4 4.3 %copy-start.4 = (bf16[512,512]{1,0:T(8,128)(2,1)S(1)}, bf16[512,512]{1,0:T(8,128)(2,1)}, u32[]{:S(2)}) copy-start(bf16[512,512]{1,0:T(8,128)(2,1)} %get-tuple-element.22) | copy-start | bytes 1572868
  172.8 1.5 copy-start.5
  174.4 3.0 %copy-start = (bf16[512,1280]{1,0:T(8,128)(2,1)S(1)}, bf16[512,1280]{1,0:T(8,128)(2,1)}, u32[]{:S(2)}) copy-start(bf16[512,1280]{1,0:T(8,128)(2,1)} %get-tuple-element.24) | copy-start | bytes 3932164
  177.3 1.6 copy-start.2
  177.3 2.4 %copy-start.1 = (f32[480,256]{1,0:T(8,128)S(1)}, f32[480,256]{1,0:T(8,128)}, u32[]{:S(2)}) copy-start(f32[480,256]{1,0:T(8,128)} %get-tuple-element.69) | copy-start | bytes 1474564
where the time goes:
time: 182 us; the launch traced here: 180 us
  Pallas kernels  162 us (89%)
  other arithmetic  10.3 us (6%)
  local copies, waits for them, and re-layouts  7.32 us (4%)
    pallas_call x1, Pallas kernels, run_layer(): pl.pallas_call(mega_kernel, out_shape=[jax.ShapeDtypeStruct((BLOCK, 256),...  162 us
    convert_element_type x3, other arithmetic, on_device(): f32 = {name: v[:BLOCK].astype(jnp.float32) for name, v in zip(NAMES, sums)}  5.98 us
    unnamed x24, local copies, waits for them, and re-layouts  5.51 us

commit v1 on v0

--- a/solution.py
+++ b/solution.py
@@ -181,7 +181,6 @@
     grad_gain = [jnp.sum(grad[r] * resid[r] * scale, axis=1, keepdims=True) for r in range(2)]
     return grad_resid, grad_gain
 
-UNIT = 48
 BLOCK = 480
 QKV = 896
 NAMES = [s[0] for s in STREAMS]
@@ -206,13 +205,13 @@
     (
         seq_in, seq_own, misc_all, tok_all, cot_all, n1t, flat, qkvt, q_rot, k_rot, v_rot, probs_ref,
         ctxt, midt, n2t, gate_ref, up_ref, hidden, gbt, g_gate, g_up, g_midt,
-        gat, gan, g_ctx, g_qkvt, out_own, scales,
-    ) = refs[:28]
+        gat, gan, g_ctx, g_qkvt, out_own, scales, cot_out, cot_low, cot_got,
+    ) = refs[:31]
     work = qkvt.at[0:D]
     (
         local_sem, x_send, x_recv, relay_send, relay_recv, wm_send, wm_recv, act_send, act_recv,
-        mate_send, mate_recv, rs_send, rs_recv, ag_send, ag_recv, keep_sem, end_send, end_recv,
-    ) = refs[28:]
+        mate_send, mate_recv, rs_recv, ag_recv, keep_sem, end_send, end_recv, out_sem, ring_recv, last_recv,
+    ) = refs[31:]
     acc["out"] = w_up.at[:, 0:ROWS, 0:512]
     acc["q"] = w_up.at[:, 0:ROWS, 512:1024]
     stage = {
@@ -239,9 +238,14 @@
         lead, base = (row, col) if i == 1 else (col, row)
         return full[i].at[lead, pl.ds(aligned(base * BLOCK, 16), BLOCK)]
 
-    def part(i, row, col, unit):
+    def part(i, row, col, start, count):
         lead, base = (row, col) if i == 1 else (col, row)
-        return full[i].at[lead, pl.ds(aligned(base * BLOCK + unit * UNIT, 16), UNIT)]
+        return full[i].at[lead, pl.ds(aligned(base * BLOCK + start, 16), count)]
+
+    near, far = 1 + 2 * r, 3 - 2 * r
+    x_parts = (
+        (far, place["y"] * 64, 64), (near, 256 + place["z"] * 48, 48), (far, 448, 16), (near, 464, 16)
+    )
 
     late = []
     seq_copy = send(seq, seq_in, act_send.at[2], act_recv.at[2], diagonal)
@@ -258,41 +262,50 @@
 
     tok_local = local(tok.at[:, mine], tok_all.at[r], local_sem.at[k])
     cot_local = local(cot.at[:, mine], cot_all.at[r], local_sem.at[k + 1])
+    cot_theirs = local(cot.at[:, theirs], cot_out, local_sem.at[k + 3])
     misc_local = local(misc, misc_all.at[r], local_sem.at[k + 2])
     x_in, w_local, w_mate = [], [], []
+
+    def to_x(i, j):
+        step, start, count = x_parts[j]
+        return send(
+            src[i].at[pl.ds(aligned(start, 16), count)], part(i, r, c, start, count), x_send.at[i, j],
+            x_recv.at[i, j], device(place, "x", step),
+        )
+
     for i in range(k):
         arrive = []
-        for j, (step, unit) in enumerate(((1, place["y"]), (3, 4 + place["z"]), (1, 8), (3, 9))):
-            rows = pl.ds(aligned(unit * UNIT, 16), UNIT)
-            arrive.append(
-                send(
-                    src[i].at[rows], part(i, r, c, unit), x_send.at[i, j], x_recv.at[i, j],
-                    device(place, "x", step),
-                )
-            )
+        for j in range(2):
+            arrive.append(to_x(i, j))
         x_in.append(arrive)
         w_local.append(local(src[i], spot(i, r, c), local_sem.at[i]))
         w_mate.append(send(src[i], spot(i, r, c), wm_send.at[i, 0], wm_recv.at[i, 0], core_mate))
-    cot_copy = send(cot.at[:, theirs], cot_all.at[r], act_send.at[1], act_recv.at[1], row_mate)
 
     relays, forwards = {}, {}
 
+    def pass_on(i, axis, start, count, d, slot):
+        piece = part(i, 1 - r, c, start, count)
+        return send(
+            piece, piece, relay_send.at[i, slot], relay_recv.at[i, slot], device(place, axis, d)
+        )
+
     def relay(i):
-        copies = []
-        for j, (axis, unit) in enumerate((("y", place["y"]), ("z", 4 + place["z"]))):
-            x_in[i][j].wait_recv()
-            piece = part(i, 1 - r, c, unit)
-            for d in (2, 1, 3):
-                copies.append(
-                    send(
-                        piece, piece, relay_send.at[i, j, d - 1], relay_recv.at[i, j, d - 1],
-                        device(place, axis, d),
-                    )
-                )
-        relays[i] = copies
+        x_in[i][0].wait_recv()
+        relays[i] = [pass_on(i, "y", place["y"] * 64, 64, d, slot) for slot, d in ((0, 1), (1, 3))]
+        x_in[i][1].wait_recv()
+        relays[i] += [
+            pass_on(i, "z", 256 + place["z"] * 48, 48, d, slot) for slot, d in ((2, 2), (3, 1), (4, 3))
+        ]
+        x_in[i] += [to_x(i, 2), to_x(i, 3)]
+
+    def relay_on(i):
+        relays[i][0].wait_recv()
+        relays[i].append(pass_on(i, "y", (place["y"] + 3) % 4 * 64, 32, 1, 5))
+        relays[i][1].wait_recv()
+        relays[i].append(pass_on(i, "y", (place["y"] + 1) % 4 * 64 + 32, 32, 3, 6))
 
     def forward(i):
-        for copy in x_in[i][2:] + relays[i]:
+        for copy in x_in[i][2:] + relays[i][2:]:
             copy.wait_recv()
         block = spot(i, 1 - r, c)
         forwards[i] = send(block, block, wm_send.at[i, 1], wm_recv.at[i, 1], core_mate)
@@ -318,7 +331,7 @@
         flying[name] = [
             send(
                 streams[name].piece(acc[name], level, (place[axis] + d) % 4), got[name][level].at[d - 1],
-                rs_send.at[i, level, d - 1], rs_recv.at[i, level, d - 1], device(place, axis, d),
+                out_sem.at[i, d - 1], rs_recv.at[i, level - 1, d - 1], device(place, axis, d),
             )
             for d in (2, 1, 3)
         ]
@@ -328,27 +341,64 @@
         there = streams[name].result(result[name], level)
         flying[name] = [
             send(
-                there if source is None else source, there, ag_send.at[i, level, d - 1],
-                ag_recv.at[i, level, d - 1], device(place, axis, d),
+                there if source is None else source, there, out_sem.at[i, d - 1],
+                ag_recv.at[i, level - 1, d - 1] if level else last_recv.at[i, 0, 0], device(place, axis, d),
             )
             for d in ((2,) if axis == "x" else (2, 1, 3))
         ]
+
+    def half_of(name, owner, side):
+        if streams[name].order[0] == "x":
+            return acc[name].at[owner % 2, pl.ds(aligned(owner // 2 * 256 + side * 128, 16), 128)]
+        return acc[name].at[side, pl.ds(aligned(owner * 128, 16), 128)]
+
+    def ring(name, slot, source, step):
+        i, axis = NAMES.index(name), streams[name].order[0]
+        return send(
+            source, got[name][0].at[slot], out_sem.at[i, slot], ring_recv.at[i, slot], device(place, axis, step)
+        )
 
     def advance(name):
         step = level_of.get(name, 0)
         level_of[name] = step + 1
         i = NAMES.index(name)
+        axis = streams[name].order[0]
+        me = place[axis]
+        after, across, before = [(me + d) % 4 for d in (1, 2, 3)]
         if step == 0:
             mates[name].wait_recv()
             for lead in range(2):
                 theirs = mate[name].at[lead if name == "down" else pl.ds(lead * BLOCK, BLOCK)]
                 add_rows(acc[name].at[lead, 0:BLOCK], [theirs])
-            scatter(name, 0)
+            flying[name] = [
+                ring(name, 0, half_of(name, across, 0), 1),
+                ring(name, 1, half_of(name, across, 1), 3),
+                ring(name, 2, half_of(name, after, 1), 1),
+                ring(name, 3, half_of(name, before, 0), 3),
+            ]
+            return
+        if step == 1:
+            for copy, owner, side in ((flying[name][0], after, 0), (flying[name][1], before, 1)):
+                copy.wait_recv()
+                add_rows(half_of(name, owner, side), [got[name][0].at[side]])
+            flying[name] += [
+                ring(name, 4, half_of(name, after, 0), 1),
+                ring(name, 5, half_of(name, before, 1), 3),
+            ]
+            return
+        if step == 2:
+            for copy in flying[name][:2]:
+                copy.wait_send()
+            for copy in flying[name][2:]:
+                copy.wait()
+            add_rows(half_of(name, me, 0), [got[name][0].at[3], got[name][0].at[4]])
+            add_rows(half_of(name, me, 1), [got[name][0].at[2], got[name][0].at[5]])
+            scatter(name, 1)
             return
         for copy in flying[name]:
             copy.wait()
-        if step <= 3:
-            level = step - 1
+        if step <= 4:
+            level = step - 2
             own = streams[name].piece(acc[name], level, place[streams[name].order[level]])
             add_rows(own, [got[name][level].at[d] for d in range(3)])
             if level < 2:
@@ -356,10 +406,26 @@
             else:
                 keep[name] = local(own, streams[name].result(result[name], 2), keep_sem.at[i])
                 spread(name, 2, own)
-        elif step <= 5:
-            if step == 4:
-                keep[name].wait()
-            spread(name, 5 - step)
+        elif step == 5:
+            keep[name].wait()
+            spread(name, 1)
+        elif step == 6 and axis == "x":
+            spread(name, 0)
+        elif step in (6, 7) and axis != "x":
+            base = [aligned(p * 128, 16) for p in (me, before, after)]
+            if step == 6:
+                pieces = [pl.ds(base[0], 128)] * 2
+            else:
+                pieces = [pl.ds(base[1], 64), pl.ds(base[2] + 64, 64)]
+            flying[name] = [
+                send(
+                    result[name].at[rows], result[name].at[rows], out_sem.at[i, d // 2],
+                    last_recv.at[i, step - 6, d // 2], device(place, axis, d),
+                )
+                for rows, d in zip(pieces, (1, 3))
+            ]
+        else:
+            flying[name] = []
 
     def wgrad(left, right_of, name, columns=256):
         n = N_OF[name]
@@ -418,17 +484,25 @@
     for row in two:
         n1t[rows_of[row], :] = low(resid(row) * scales[0:1, :] * gain_one[row])
     flat[...] = n1t[...].T
+    relay_on(0)
     relay(2)
+    relay_on(1)
+    relay(3)
     forward(0)
-    relay(3)
+    relay(4)
+    relay_on(2)
+    cot_theirs.wait()
+    cot_low[...] = low(cot_out[...])
+    cot_copy = send(cot_low, cot_got, act_send.at[1], act_recv.at[1], row_mate)
     ready(0)
     for col in two:
         both = nn(flat[...], w_qkv[col]).T
         qkvt[col * BLOCK : col * BLOCK + BLOCK, :] = both[:BLOCK]
         qkvt[960 + col * 160 : 1120 + col * 160, :] = both[480:640]
         qkvt[1280 + col * 160 : 1440 + col * 160, :] = both[640:800]
-    relay(4)
     forward(1)
+    relay_on(3)
+    relay_on(4)
     for h in range(KVH):
         k_rot[h * 64 : h * 64 + 64, :] = low(rotate(qkvt[960 + h * 64 : 1024 + h * 64, :], cosine, sine))
         v_rot[h * 64 : h * 64 + 64, :] = low(qkvt[1280 + h * 64 : 1344 + h * 64, :])
@@ -474,6 +548,7 @@
 
     cot_local.wait()
     cot_copy.wait()
+    cot_all[1 - r] = cot_got[...].astype(jnp.float32)
     for row in two:
         gbt[rows_of[row], :] = low(cot_all[row])
     flat[...] = gbt[...].T
@@ -594,9 +669,9 @@
     g_tok_ref[:, mine] = g_midt[pl.ds(aligned(r * BLOCK, 16), BLOCK), :]
     advance("q")
     advance("kv")
-    while any(level_of[name] < 7 for name in NAMES):
+    while any(level_of[name] < 9 for name in NAMES):
         for name in NAMES:
-            if level_of[name] < 7:
+            if level_of[name] < 9:
                 advance(name)
     out_copy.wait()
     g_copy.wait()
@@ -620,7 +695,7 @@
     scratch += [v((2, BLOCK, n) if name == "down" else (2 * BLOCK, n)) for name, n, _ in STREAMS]
     for _, n, order in STREAMS:
         for level in range(3):
-            scratch.append(v((3,) + Stream(order, place).shape(level, n)))
+            scratch.append(v((3,) + Stream(order, place).shape(level, n) if level else (6, 128, n)))
     scratch += [
         v((8, 128), jnp.int32), v((8, 128), jnp.int32), v((2, 8, 512), f32), v((2, BLOCK, 128)),
         v((2, BLOCK, 128), f32), v((D, 128)), v((128, D)), v((1600, 128), f32), v((320, 384)),
@@ -628,12 +703,12 @@
         v((D, 128)), v((2, 128, 1280), f32), v((2, 128, 1280), f32), v((2, 128, 1280)),
         v((D, 128)), v((2, 128, 1280)), v((2, 128, 1280)),
         v((D, 128), f32), v((992, 128)), v((2, 128, 512)), v((D, 128)), v((2, QKV, 128)), v((D, 128), f32),
-        v((8, 128), f32),
+        v((8, 128), f32), v((BLOCK, 128), f32), v((BLOCK, 128)), v((BLOCK, 128)),
     ]
     scratch += [
-        dma((8,)), dma((5, 4)), dma((5, 4)), dma((5, 2, 3)), dma((5, 2, 3)), dma((5, 2)), dma((5, 2)),
-        dma((4,)), dma((4,)), dma((6,)), dma((6,)), dma((6, 3, 3)), dma((6, 3, 3)), dma((6, 3, 3)),
-        dma((6, 3, 3)), dma((6,)), dma((2,)), dma((2,)),
+        dma((9,)), dma((5, 4)), dma((5, 4)), dma((5, 7)), dma((5, 7)), dma((5, 2)), dma((5, 2)),
+        dma((4,)), dma((4,)), dma((6,)), dma((6,)), dma((6, 2, 3)), dma((6, 2, 3)),
+        dma((6,)), dma((2,)), dma((2,)), dma((6, 6)), dma((6, 6)), dma((6, 2, 2)),
     ]
     return pl.pallas_call(
         mega_kernel,
@@ -649,6 +724,39 @@
     )(*weights, tokens, cotangent, seq, misc)
 
 
+def widen_kernel(down, gate, up, out, q, kv, y, g, o_down, o_gate, o_up, o_out, o_q, o_k, o_v, o_one, o_two, o_y, o_g):
+    for a, b in ((down, o_down), (gate, o_gate), (up, o_up), (y, o_y), (g, o_g)):
+        b[...] = a[...].astype(jnp.float32)
+    for a, b in ((out, o_out), (q, o_q)):
+        b[...] = a[:, 0:480].astype(jnp.float32)
+    flipped = kv[...].astype(jnp.float32).T
+    o_k[...] = flipped[0:160]
+    o_v[...] = flipped[160:320]
+    o_one[...] = flipped[320:321]
+    o_two[...] = flipped[321:322]
+
+
+def widen(sums, out, g_tok):
+    f32 = jnp.float32
+
+    def rows(n):
+        return pl.BlockSpec((128, n), lambda i: (i, 0))
+
+    def lanes(n):
+        return pl.BlockSpec((n, 128), lambda i: (0, i))
+
+    shapes = [(BLOCK, 1280)] * 3 + [(BLOCK, 480)] * 2 + [(160, BLOCK)] * 2 + [(1, BLOCK)] * 2 + [(BLOCK, 256)] * 2
+    return pl.pallas_call(
+        widen_kernel,
+        grid=(4,),
+        out_shape=[jax.ShapeDtypeStruct(s, f32) for s in shapes],
+        in_specs=[rows(n) for _, n, _ in STREAMS] + [rows(256)] * 2,
+        out_specs=[rows(s[1]) for s in shapes[:5]] + [lanes(160)] * 2 + [lanes(1)] * 2 + [rows(256)] * 2,
+        compiler_params=pltpu.CompilerParams(vmem_limit_bytes=60 * MIB),
+        cost_estimate=pl.CostEstimate(flops=0, bytes_accessed=16 * MIB, transcendentals=0),
+    )(*sums, out, g_tok)
+
+
 def on_device(
     tokens, gain_attn, gain_mlp, w_query, w_key, w_value, w_out, w_gate, w_up, w_down, seq_lengths, cotangent
 ):
@@ -657,11 +765,9 @@
     blank = jnp.zeros((BLOCK, QKV - 800), jnp.bfloat16)
     w_qkv = jnp.concatenate([w_query, w_key, w_value, blank], axis=1)
     out, g_tok, *sums = run_layer([w_qkv, w_out, w_gate, w_up, w_down], tokens, cotangent, seq, misc)
-    f32 = {name: v[:BLOCK].astype(jnp.float32) for name, v in zip(NAMES, sums)}
+    down, gate, up, g_out, query, key, value, one, two, out, g_tok = widen(sums, out, g_tok)
     return (
-        out, g_tok, f32["kv"][:, 320], f32["kv"][:, 321],
-        f32["q"][:, :480], f32["kv"][:, :160], f32["kv"][:, 160:320], f32["out"][:, :480],
-        f32["gate"], f32["up"], f32["down"],
+        out, g_tok, one.reshape(BLOCK), two.reshape(BLOCK), query, key.T, value.T, g_out, gate, up, down
     )
 
 def solution(mesh):

time: 182 us -> 162 us (0.89)
  Pallas kernels: 162 us -> 154 us
  other arithmetic: 10.3 us -> 3.52 us
  local copies, waits for them, and re-layouts: 7.32 us -> 3.43 us
    pallas_call x1, Pallas kernels: 162 us -> 147 us  [run_layer(): pl.pallas_call(mega_kernel, out_shape=[jax.ShapeDtypeStruct((BLOCK, 256),...]
    pallas_call x0 -> x1, Pallas kernels: none -> 7.4 us  [widen(): pl.pallas_call(widen_kernel, grid=(4,), out_shape=[jax.ShapeDtypeStruct(s...]
    convert_element_type x3 -> x0, other arithmetic: 5.98 us -> none  [on_device(): f32 = {name: v[:BLOCK].astype(jnp.float32) for name, v in zip(NAMES, sums)}]
    unnamed x24 -> x2, local copies, waits for them, and re-layouts: 5.51 us -> 2.09 us
where the time goes in v1:
time: 162 us
  Pallas kernels  154 us (95%)
  other arithmetic  3.52 us (2%)
  local copies, waits for them, and re-layouts  3.43 us (2%)
    pallas_call x1, Pallas kernels, run_layer(): pl.pallas_call(mega_kernel, out_shape=[jax.ShapeDtypeStruct((BLOCK, 256),...  147 us
    pallas_call x1, Pallas kernels, widen(): pl.pallas_call(widen_kernel, grid=(4,), out_shape=[jax.ShapeDtypeStruct(s...  7.4 us

profile of v1, /device:TPU:0, one launch (start us, length us, event | category | flops | bytes accessed | tf_op | source)
XLA Modules:
  0.0 162.0 jit_solution(9912893843674139683)
XLA Ops:
  0.7 0.1 pad.15.clone
  0.7 1.3 pad.8.refs_7_
  2.0 1.3 select_maximum_fusion.refs_8_
  3.3 1.0 copy.23
  4.3 1.0 copy.24
  5.4 2.2 %maximum_maximum_fusion.refs_0_ = bf16[480,896]{1,0:T(8,128)(2,1)} fusion(bf16[480,160]{1,0:T(8,128)(2,1)S(1)} %copy.24, bf16[480,160]{1,0:T(8,128)(2,1)S(1)} %copy.23, bf16[480,480]{1,0:T(8,128)(2,1)} %param.15, bf16[896]{0:T(1024)(128)(2,1)S(1)} %pad.15.clone), kind=kLoop, calls=%fused_computation | loop fusion | flops 3440640 | bytes 1629952 | tf_op jit(solution)/shard_map/concatenate | solution.py:766
  7.6 146.9 %shard_map.203 = (f32[480,256]{1,0:T(8,128)}, f32[480,256]{1,0:T(8,128)}, bf16[512,1280]{1,0:T(8,128)(2,1)}, bf16[512,1280]{1,0:T(8,128)(2,1)}, bf16[512,1280]{1...) custom-call(bf16[480,896]{1,0:T(8,128)(2,1)} %maximum_maximum_fusion.refs_0_, ...), custom_call_target="tpu_custom_call" | custom-call | flops 8000000000 | bytes 62914560 | tf_op jit(solution)/shard_map/pallas_call | solution.py:713
  154.5 7.4 %shard_map.204 = (f32[480,1280]{1,0:T(8,128)}, f32[480,1280]{1,0:T(8,128)}, f32[480,1280]{1,0:T(8,128)}, f32[480,480]{1,0:T(8,128)}, f32[480,480]{1,0:T(8,128)},...) custom-call(bf16[512,1280]{1,0:T(8,128)(2,1)} %get-tuple-element.30., ...), custom_call_target="tpu_custom_call" | custom-call | bytes 16777216 | tf_op jit(solution)/shard_map/pallas_call | solution.py:749
  (1 shorter events, 0.0 us)

commit v2 on v1

--- a/solution.py
+++ b/solution.py
@@ -45,9 +45,12 @@
 
 ROWS = 512
 STREAMS = (
-    ("down", 1280, "xyz"),
-    ("gate", 1280, "yzx"),
-    ("up", 1280, "zxy"),
+    ("down0", 640, "xyz"),
+    ("down1", 640, "xyz"),
+    ("gate0", 640, "yzx"),
+    ("gate1", 640, "yzx"),
+    ("up0", 640, "zxy"),
+    ("up1", 640, "zxy"),
     ("out", 512, "xyz"),
     ("q", 512, "yzx"),
     ("kv", 384, "zxy"),
@@ -185,39 +188,45 @@
 QKV = 896
 NAMES = [s[0] for s in STREAMS]
 N_OF = {s[0]: s[1] for s in STREAMS}
+TAIL = ("q", "kv", "down0")
+ORDER = ("gate1", "up1", "down0", "gate0", "up0", "down1", "out", "q", "kv")
+OWN_SPACE = NAMES[:6] + ["kv"]
 
 
 def mega_kernel(*refs):
     k = 5
-    src = refs[:k]
-    tok, cot, seq, misc = refs[k : k + 4]
-    refs = refs[k + 4 :]
+    src = (None,) + refs[: k - 1]
+    tok, cot, w_query, w_key_t, w_value_t, lengths, gain_one_ref, gain_two_ref = refs[k - 1 : k + 7]
+    refs = refs[k + 7 :]
     out_ref, g_tok_ref = refs[:2]
-    result = dict(zip(NAMES, refs[2:8]))
-    refs = refs[8:]
+    result = dict(zip(NAMES, refs[2:11]))
+    refs = refs[11:]
     full, refs = refs[:k], refs[k:]
     w_qkv, w_out, w_gate, w_up, w_down = full
-    acc = dict(zip(("down", "gate", "up", "kv"), refs[:4]))
-    refs = refs[4:]
-    mate, refs = dict(zip(NAMES, refs[:6])), refs[6:]
+    acc = dict(zip(OWN_SPACE, refs[:7]))
+    refs = refs[7:]
+    mate, refs = dict(zip(NAMES, refs[:9])), refs[9:]
     got = {name: refs[3 * i : 3 * i + 3] for i, name in enumerate(NAMES)}
-    refs = refs[18:]
+    refs = refs[27:]
     (
         seq_in, seq_own, misc_all, tok_all, cot_all, n1t, flat, qkvt, q_rot, k_rot, v_rot, probs_ref,
         ctxt, midt, n2t, gate_ref, up_ref, hidden, gbt, g_gate, g_up, g_midt,
-        gat, gan, g_ctx, g_qkvt, out_own, scales, cot_out, cot_low, cot_got,
-    ) = refs[:31]
+        gat, gan, g_ctx, g_qkvt, out_own, scales, cot_out, cot_low, cot_got, seq, misc,
+    ) = refs[:33]
     work = qkvt.at[0:D]
     (
         local_sem, x_send, x_recv, relay_send, relay_recv, wm_send, wm_recv, act_send, act_recv,
         mate_send, mate_recv, rs_recv, ag_recv, keep_sem, end_send, end_recv, out_sem, ring_recv, last_recv,
-    ) = refs[31:]
+    ) = refs[33:]
     acc["out"] = w_up.at[:, 0:ROWS, 0:512]
     acc["q"] = w_up.at[:, 0:ROWS, 512:1024]
     stage = {
-        "down": acc["gate"].at[:, 0:BLOCK],
-        "gate": w_down.at[0],
-        "up": w_down.at[1],
+        "down0": acc["gate0"].at[:, 0:BLOCK],
+        "down1": acc["gate1"].at[:, 0:BLOCK],
+        "gate0": w_down.at[0, :, 0:640],
+        "gate1": w_down.at[0, :, 640:1280],
+        "up0": w_down.at[1, :, 0:640],
+        "up1": w_down.at[1, :, 640:1280],
         "out": w_gate.at[0, :, 0:512],
         "q": w_gate.at[0, :, 512:1024],
         "kv": w_gate.at[1, :, 0:384],
@@ -228,6 +237,8 @@
     t = lax.axis_index("tok")
     row_mate, diagonal = (t, 1 - r, c), (t, 1 - r, 1 - c)
     core_mate = device(place, "c", 1)
+    seq[...] = jnp.zeros((8, 128), jnp.int32)
+    misc[...] = jnp.zeros((8, 512), jnp.float32)
     barrier = pltpu.get_barrier_semaphore()
     partners = [core_mate] + [device(place, a, d) for a in "xyz" for d in (1, 2, 3)] + [diagonal]
     for target in partners:
@@ -247,7 +258,9 @@
         (far, place["y"] * 64, 64), (near, 256 + place["z"] * 48, 48), (far, 448, 16), (near, 464, 16)
     )
 
-    late = []
+    seq[0:1, 0:3] = lengths[...]
+    misc[0:1, 0:BLOCK] = gain_one_ref[...]
+    misc[1:2, 0:BLOCK] = gain_two_ref[...]
     seq_copy = send(seq, seq_in, act_send.at[2], act_recv.at[2], diagonal)
     misc_copy = send(misc, misc_all.at[r], act_send.at[3], act_recv.at[3], row_mate)
     theirs = pl.ds(aligned((1 - r) * 128, 128), 128)
@@ -268,18 +281,22 @@
 
     def to_x(i, j):
         step, start, count = x_parts[j]
+        own = part(0, r, c, start, count) if i == 0 else src[i].at[pl.ds(aligned(start, 16), count)]
         return send(
-            src[i].at[pl.ds(aligned(start, 16), count)], part(i, r, c, start, count), x_send.at[i, j],
+            own, part(i, r, c, start, count), x_send.at[i, j],
             x_recv.at[i, j], device(place, "x", step),
         )
 
+    own_rows = pl.ds(aligned(r * BLOCK, 16), BLOCK)
+    w_qkv[c, own_rows, 0:BLOCK] = w_query[...]
+    w_qkv[c, own_rows, BLOCK:QKV] = jnp.concatenate(
+        [w_key_t[...].T, w_value_t[...].T, jnp.zeros((BLOCK, QKV - 800), jnp.bfloat16)], axis=1
+    )
     for i in range(k):
-        arrive = []
-        for j in range(2):
-            arrive.append(to_x(i, j))
-        x_in.append(arrive)
-        w_local.append(local(src[i], spot(i, r, c), local_sem.at[i]))
-        w_mate.append(send(src[i], spot(i, r, c), wm_send.at[i, 0], wm_recv.at[i, 0], core_mate))
+        x_in.append([to_x(i, 0), to_x(i, 1)])
+        own = src[i] if i else spot(0, r, c)
+        w_local.append(local(own, spot(i, r, c), local_sem.at[i]) if i else None)
+        w_mate.append(send(own, spot(i, r, c), wm_send.at[i, 0], wm_recv.at[i, 0], core_mate))
 
     relays, forwards = {}, {}
 
@@ -311,7 +328,8 @@
         forwards[i] = send(block, block, wm_send.at[i, 1], wm_recv.at[i, 1], core_mate)
 
     def ready(i):
-        w_local[i].wait()
+        if i:
+            w_local[i].wait()
         w_mate[i].wait_recv()
         forwards[i].wait_recv()
 
@@ -368,7 +386,7 @@
         if step == 0:
             mates[name].wait_recv()
             for lead in range(2):
-                theirs = mate[name].at[lead if name == "down" else pl.ds(lead * BLOCK, BLOCK)]
+                theirs = mate[name].at[lead if name[:4] == "down" else pl.ds(lead * BLOCK, BLOCK)]
                 add_rows(acc[name].at[lead, 0:BLOCK], [theirs])
             flying[name] = [
                 ring(name, 0, half_of(name, across, 0), 1),
@@ -427,26 +445,24 @@
         else:
             flying[name] = []
 
-    def wgrad(left, right_of, name, columns=256):
-        n = N_OF[name]
-        steps = -(-n // columns)
-
-        def block(col, lanes, row):
-            return low(nn(left[row * BLOCK : row * BLOCK + BLOCK, :], right_of(col, lanes)))
+    def wgrad(left, right, name):
+        first = 640 * int(name[-1])
 
         def run(col, put):
-            if n % columns == 0:
-                @pl.loop(0, steps)
-                def _(j):
-                    lanes = pl.ds(aligned(j * columns, columns), columns)
-                    for row in range(2):
-                        put(row, lanes, block(col, lanes, row))
-            else:
+            def chunk(start, count):
+                lanes = pl.ds(aligned(first + start, 128), count)
                 for row in range(2):
-                    put(row, pl.ds(0, n), block(col, pl.ds(0, n), row))
+                    rows = slice(row * BLOCK, row * BLOCK + BLOCK)
+                    put(row, pl.ds(aligned(start, 128), count), low(nn(left[rows, :], right[col, :, lanes])))
+
+            @pl.loop(0, 2)
+            def _(j):
+                chunk(j * 256, 256)
+
+            chunk(512, 128)
 
         def put_stage(row, lanes, value):
-            if name == "down":
+            if name[:4] == "down":
                 stage[name][row, :, lanes] = value
             else:
                 stage[name][row * BLOCK : row * BLOCK + BLOCK, lanes] = value
@@ -456,9 +472,11 @@
 
         run(1 - c, put_stage)
         to_mate(name)
+        yield
         run(c, put_acc)
         for row in range(2):
-            acc[name][row, BLOCK:ROWS, :] = jnp.zeros((ROWS - BLOCK, n), jnp.bfloat16)
+            acc[name][row, BLOCK:ROWS, :] = jnp.zeros((ROWS - BLOCK, 640), jnp.bfloat16)
+        yield
 
     two = range(2)
     rows_of = [slice(row * BLOCK, row * BLOCK + BLOCK) for row in two]
@@ -552,7 +570,8 @@
     for row in two:
         gbt[rows_of[row], :] = low(cot_all[row])
     flat[...] = gbt[...].T
-    wgrad(gbt, lambda col, lanes: hidden[col, :, lanes], "down")
+    for _ in zip(wgrad(gbt, hidden, "down0"), wgrad(gbt, hidden, "down1")):
+        pass
     ready(4)
 
     @pl.loop(0, 10)
@@ -565,7 +584,8 @@
         g_gate[col, :, lanes] = low(grad * up_ref[col, :, lanes] * sig * (1.0 + gate * (1.0 - sig)))
         g_up[col, :, lanes] = low(grad * (gate * sig))
 
-    advance("down")
+    advance("down0")
+    advance("down1")
     work[...] = midt[...]
     for col in two:
         work[...] += nt(w_down[col], hidden[col])
@@ -576,13 +596,28 @@
     )
     out_ref[:, mine] = out_own[pl.ds(aligned(r * BLOCK, 16), BLOCK), :]
     release(4)
-    mates["down"].wait_send()
-    wgrad(n2t, lambda col, lanes: g_gate[col, :, lanes], "gate")
-    wgrad(n2t, lambda col, lanes: g_up[col, :, lanes], "up")
-    advance("gate")
+    mates["down0"].wait_send()
+    mates["down1"].wait_send()
+    works = [
+        wgrad(n2t, right, name)
+        for name, right in (("gate0", g_gate), ("up0", g_up), ("gate1", g_gate), ("up1", g_up))
+    ]
+    next(works[0])
+    next(works[1])
+    next(works[0])
+    next(works[1])
+    next(works[2])
+    next(works[3])
+    advance("gate0")
+    advance("up0")
+    next(works[2])
+    next(works[3])
+    advance("down0")
     work[...] = nt(w_gate[0], g_gate[0]) + nt(w_gate[1], g_gate[1])
-    advance("up")
+    advance("gate1")
+    advance("up1")
     work[...] += nt(w_up[0], g_up[0]) + nt(w_up[1], g_up[1])
+    advance("down1")
     release(2)
     release(3)
     back, gain_two_grad = norm_back(
@@ -610,7 +645,8 @@
     for row in two:
         acc["out"][row, 0:BLOCK, :] = out_block(c, row)
         acc["out"][row, BLOCK:ROWS, :] = jnp.zeros((ROWS - BLOCK, 512), jnp.bfloat16)
-    advance("down")
+    advance("gate0")
+    advance("up0")
     for h in range(KVH):
         own = slice(h * 64, h * 64 + 64)
         g_cat = jnp.concatenate(
@@ -631,10 +667,6 @@
                 row = at + 32 * half
                 put = base + row % width
                 g_qkvt[row // width, put : put + 32, :] = value[half * 32 : half * 32 + 32]
-        if h == 1:
-            advance("gate")
-        if h == 2:
-            advance("up")
     for col in two:
         g_qkvt[col, 800:QKV, :] = jnp.zeros((QKV - 800, 128), jnp.bfloat16)
     advance("out")
@@ -667,21 +699,21 @@
         end_recv.at[1], row_mate,
     )
     g_tok_ref[:, mine] = g_midt[pl.ds(aligned(r * BLOCK, 16), BLOCK), :]
-    advance("q")
-    advance("kv")
+    for name in TAIL:
+        advance(name)
     while any(level_of[name] < 9 for name in NAMES):
-        for name in NAMES:
+        for name in ORDER:
             if level_of[name] < 9:
                 advance(name)
     out_copy.wait()
     g_copy.wait()
-    for name in NAMES[1:]:
+    for name in NAMES[2:]:
         mates[name].wait_send()
     release(0)
     release(1)
 
 
-def run_layer(weights, tokens, cotangent, seq, misc):
+def run_layer(weights, tokens, cotangent, w_query, w_key_t, w_value_t, lengths, gain_one, gain_two):
     bf, f32 = jnp.bfloat16, jnp.float32
     dma = pltpu.SemaphoreType.DMA
     hbm, vmem = pl.BlockSpec(memory_space=pl.ANY), pl.BlockSpec(memory_space=pltpu.VMEM)
@@ -690,9 +722,9 @@
     def v(shape, dtype=bf):
         return pltpu.VMEM(shape, dtype)
 
-    scratch = [v((2, 2 * BLOCK, w.shape[1])) for w in weights]
-    scratch += [v((2, ROWS, N_OF[name])) for name in ("down", "gate", "up", "kv")]
-    scratch += [v((2, BLOCK, n) if name == "down" else (2 * BLOCK, n)) for name, n, _ in STREAMS]
+    scratch = [v((2, 2 * BLOCK, QKV))] + [v((2, 2 * BLOCK, w.shape[1])) for w in weights]
+    scratch += [v((2, ROWS, N_OF[name])) for name in OWN_SPACE]
+    scratch += [v((2, BLOCK, n) if name[:4] == "down" else (2 * BLOCK, n)) for name, n, _ in STREAMS]
     for _, n, order in STREAMS:
         for level in range(3):
             scratch.append(v((3,) + Stream(order, place).shape(level, n) if level else (6, 128, n)))
@@ -703,30 +735,37 @@
         v((D, 128)), v((2, 128, 1280), f32), v((2, 128, 1280), f32), v((2, 128, 1280)),
         v((D, 128)), v((2, 128, 1280)), v((2, 128, 1280)),
         v((D, 128), f32), v((992, 128)), v((2, 128, 512)), v((D, 128)), v((2, QKV, 128)), v((D, 128), f32),
-        v((8, 128), f32), v((BLOCK, 128), f32), v((BLOCK, 128)), v((BLOCK, 128)),
+        v((8, 128), f32), v((BLOCK, 128), f32), v((BLOCK, 128)), v((BLOCK, 128)), v((8, 128), jnp.int32),
+        v((8, 512), f32),
     ]
     scratch += [
         dma((9,)), dma((5, 4)), dma((5, 4)), dma((5, 7)), dma((5, 7)), dma((5, 2)), dma((5, 2)),
-        dma((4,)), dma((4,)), dma((6,)), dma((6,)), dma((6, 2, 3)), dma((6, 2, 3)),
-        dma((6,)), dma((2,)), dma((2,)), dma((6, 6)), dma((6, 6)), dma((6, 2, 2)),
+        dma((4,)), dma((4,)), dma((9,)), dma((9,)), dma((9, 2, 3)), dma((9, 2, 3)), dma((9,)), dma((2,)), dma((2,)),
+        dma((9, 6)), dma((9, 6)), dma((9, 2, 2)),
     ]
     return pl.pallas_call(
         mega_kernel,
         out_shape=[jax.ShapeDtypeStruct((BLOCK, 256), f32)] * 2
         + [jax.ShapeDtypeStruct((ROWS, n), bf) for _, n, _ in STREAMS],
-        in_specs=[hbm] * 7 + [vmem] * 2,
-        out_specs=[vmem] * 2 + [hbm] * 6,
+        in_specs=[hbm] * 6 + [vmem] * 6,
+        out_specs=[vmem] * 2 + [hbm] * 9,
         scratch_shapes=scratch,
         compiler_params=pltpu.CompilerParams(
             collective_id=1, has_side_effects=True, vmem_limit_bytes=63 * MIB
         ),
         cost_estimate=pl.CostEstimate(flops=8 * 10**9, bytes_accessed=60 * MIB, transcendentals=0),
-    )(*weights, tokens, cotangent, seq, misc)
-
-
-def widen_kernel(down, gate, up, out, q, kv, y, g, o_down, o_gate, o_up, o_out, o_q, o_k, o_v, o_one, o_two, o_y, o_g):
-    for a, b in ((down, o_down), (gate, o_gate), (up, o_up), (y, o_y), (g, o_g)):
-        b[...] = a[...].astype(jnp.float32)
+    )(*weights, tokens, cotangent, w_query, w_key_t, w_value_t, lengths, gain_one, gain_two)
+
+
+def widen_kernel(
+    down0, down1, gate0, gate1, up0, up1, out, q, kv, y, g,
+    o_down, o_gate, o_up, o_out, o_q, o_k, o_v, o_one, o_two, o_y, o_g
+):
+    for a, b, whole in ((down0, down1, o_down), (gate0, gate1, o_gate), (up0, up1, o_up)):
+        whole[:, 0:640] = a[...].astype(jnp.float32)
+        whole[:, 640:1280] = b[...].astype(jnp.float32)
+    o_y[...] = y[...]
+    o_g[...] = g[...]
     for a, b in ((out, o_out), (q, o_q)):
         b[...] = a[:, 0:480].astype(jnp.float32)
     flipped = kv[...].astype(jnp.float32).T
@@ -760,11 +799,10 @@
 def on_device(
     tokens, gain_attn, gain_mlp, w_query, w_key, w_value, w_out, w_gate, w_up, w_down, seq_lengths, cotangent
 ):
-    seq = jnp.pad(seq_lengths, ((0, 7), (0, 125)))
-    misc = jnp.pad(jnp.stack([gain_attn, gain_mlp]), ((0, 6), (0, 32)))
-    blank = jnp.zeros((BLOCK, QKV - 800), jnp.bfloat16)
-    w_qkv = jnp.concatenate([w_query, w_key, w_value, blank], axis=1)
-    out, g_tok, *sums = run_layer([w_qkv, w_out, w_gate, w_up, w_down], tokens, cotangent, seq, misc)
+    out, g_tok, *sums = run_layer(
+        [w_out, w_gate, w_up, w_down], tokens, cotangent, w_query, w_key.T, w_value.T, seq_lengths,
+        gain_attn.reshape(1, BLOCK), gain_mlp.reshape(1, BLOCK),
+    )
     down, gate, up, g_out, query, key, value, one, two, out, g_tok = widen(sums, out, g_tok)
     return (
         out, g_tok, one.reshape(BLOCK), two.reshape(BLOCK), query, key.T, value.T, g_out, gate, up, down

time: 162 us -> 153 us (0.944)
  other arithmetic: 3.52 us -> 0 us
  local copies, waits for them, and re-layouts: 3.43 us -> 0 us
  Pallas kernels: 154 us -> 152 us
    pallas_call x1, Pallas kernels: 147 us -> 145 us  [run_layer(): pl.pallas_call(mega_kernel, out_shape=[jax.ShapeDtypeStruct((BLOCK, 256),...]
    concatenate x1 -> x0, other arithmetic: 2.2 us -> none  [on_device(): w_qkv = jnp.concatenate([w_query, w_key, w_value, blank], axis=1)]
    unnamed x2 -> x0, local copies, waits for them, and re-layouts: 2.09 us -> none
where the time goes in v2:
time: 153 us
  Pallas kernels  152 us (99%)
    pallas_call x1, Pallas kernels, run_layer(): pl.pallas_call(mega_kernel, out_shape=[jax.ShapeDtypeStruct((BLOCK, 256),...  145 us
    pallas_call x1, Pallas kernels, widen(): pl.pallas_call(widen_kernel, grid=(4,), out_shape=[jax.ShapeDtypeStruct(s...  7.35 us

profile of v2, /device:TPU:0, one launch (start us, length us, event | category | flops | bytes accessed | tf_op | source)
XLA Modules:
  0.0 152.8 jit_solution(3747749458518436637)
XLA Ops:
  0.6 144.6 %shard_map.203 = (f32[480,256]{1,0:T(8,128)}, f32[480,256]{1,0:T(8,128)}, bf16[512,640]{1,0:T(8,128)(2,1)}, bf16[512,640]{1,0:T(8,128)(2,1)}, bf16[512,640]{1,0:...) custom-call(bf16[480,480]{1,0:T(8,128)(2,1)} %refs_0_.1, ...), custom_call_target="tpu_custom_call" | custom-call | flops 8000000000 | bytes 62914560 | tf_op jit(solution)/shard_map/pallas_call | solution.py:746
  145.2 7.4 %shard_map.204 = (f32[480,1280]{1,0:T(8,128)}, f32[480,1280]{1,0:T(8,128)}, f32[480,1280]{1,0:T(8,128)}, f32[480,480]{1,0:T(8,128)}, f32[480,480]{1,0:T(8,128)},...) custom-call(bf16[512,640]{1,0:T(8,128)(2,1)} %get-tuple-element.33.d, ...), custom_call_target="tpu_custom_call" | custom-call | bytes 16777216 | tf_op jit(solution)/shard_map/pallas_call | solution.py:788

commit v3 on v2

--- a/solution.py
+++ b/solution.py
@@ -102,7 +102,7 @@
         return (lead, size, n) if lead == 2 else (size, n)
 
 
-def add_rows(dst, srcs, step=16):
+def add_rows(dst, srcs, step=32):
     shape = dst.shape
     if len(shape) == 2:
         views = [(dst, srcs)]
@@ -114,6 +114,9 @@
         @pl.loop(0, rows // step)
         def _(i, d=d, ss=ss):
             at = pl.ds(aligned(i * step, step), step)
+            if len(ss) == 1:
+                d[at, :] = d[at, :] + ss[0][at, :]
+                return
             total = d[at, :].astype(jnp.float32)
             for s in ss:
                 total = total + s[at, :].astype(jnp.float32)
@@ -188,7 +191,7 @@
 QKV = 896
 NAMES = [s[0] for s in STREAMS]
 N_OF = {s[0]: s[1] for s in STREAMS}
-TAIL = ("q", "kv", "down0")
+TAIL = ("down0", "q", "kv")
 ORDER = ("gate1", "up1", "down0", "gate0", "up0", "down1", "out", "q", "kv")
 OWN_SPACE = NAMES[:6] + ["kv"]
 

time: 153 us -> 152 us (level)
  no operation moved by 1% of the time
where the time goes in v3:
time: 152 us
  Pallas kernels  151 us (99%)
    pallas_call x1, Pallas kernels, run_layer(): pl.pallas_call(mega_kernel, out_shape=[jax.ShapeDtypeStruct((BLOCK, 256),...  144 us
    pallas_call x1, Pallas kernels, widen(): pl.pallas_call(widen_kernel, grid=(4,), out_shape=[jax.ShapeDtypeStruct(s...  7.35 us

profile of v3, /device:TPU:0, one launch (start us, length us, event | category | flops | bytes accessed | tf_op | source)
XLA Modules:
  0.0 151.9 jit_solution(14469052510056575115)
XLA Ops:
  0.6 143.7 %shard_map.203 = (f32[480,256]{1,0:T(8,128)}, f32[480,256]{1,0:T(8,128)}, bf16[512,640]{1,0:T(8,128)(2,1)}, bf16[512,640]{1,0:T(8,128)(2,1)}, bf16[512,640]{1,0:...) custom-call(bf16[480,480]{1,0:T(8,128)(2,1)} %refs_0_.1, ...), custom_call_target="tpu_custom_call" | custom-call | flops 8000000000 | bytes 62914560 | tf_op jit(solution)/shard_map/pallas_call | solution.py:749
  144.4 7.4 %shard_map.204 = (f32[480,1280]{1,0:T(8,128)}, f32[480,1280]{1,0:T(8,128)}, f32[480,1280]{1,0:T(8,128)}, f32[480,480]{1,0:T(8,128)}, f32[480,480]{1,0:T(8,128)},...) custom-call(bf16[512,640]{1,0:T(8,128)(2,1)} %get-tuple-element.33.d, ...), custom_call_target="tpu_custom_call" | custom-call | bytes 16777216 | tf_op jit(solution)/shard_map/pallas_call | solution.py:791
